TPU v7x, 32 devices: a whole 2x2x4 slice. The times are simulated.
32 devices in a mesh: gx: 4 (over y, core), gy: 8 (over z, x).
Axes of the slice: x: 2, y: 2, z: 4, core: 2. Of those that a mesh axis runs over, the one named last changes fastest.
Arguments:
- pressure_init: float32 [64, 256, 128], P('gx', 'gy'), may hold values from -6 to 6
- source: float32 [64, 256, 128], P('gx', 'gy'), may hold values from -6 to 6
- permeability: float32 [64, 256, 128], P('gx', 'gy'), may hold values from 0.1 to 10
Outputs:
- pressure: float32 [64, 256, 128], P('gx', 'gy')
- correction_mid: float32 [32, 128, 128], P('gx', 'gy')
- correction_coarse: float32 [16, 64, 128], P('gx', 'gy')
All inputs are finite; a program needn't handle non-finite values.
Results may differ from a plain program's by a relative error of at most 0.0003.
Values sent between devices are 32-bit elements; how exact they have to be, the bound alone decides.
A program may use at most 64 MiB of HBM per device.

v0:
```python
import jax
import jax.numpy as jnp
from jax import lax
from jax.sharding import PartitionSpec as P

SWEEPS = 2
COARSE = 4


STORE = 0.1
OMEGA = 0.8


def with_halo(x, sides, width):
    for axis, dim in sides:
        count, length = (lax.axis_size(axis), x.shape[dim])
        up = [(i, (i + 1) % count) for i in range(count - 1)]
        down = [(j, i) for i, j in up]
        last = lax.slice_in_dim(x, length - width, length, axis=dim)
        leading = lax.slice_in_dim(x, 0, width, axis=dim)
        before = lax.ppermute(last, axis, up)
        after = lax.ppermute(leading, axis, down)
        x = jnp.concatenate([before, x, after], axis=dim)
    return x


def harmonic(first, second):
    total = first + second
    return 2.0 * first * second / jnp.where(total > 0, total, 1.0)


def widths(axis, low):
    pads = [(0, 0), (0, 0), (0, 0)]
    pads[axis] = (1, 0) if low else (0, 1)
    return pads


def face_sum(coupling, axis):
    return jnp.pad(coupling, widths(axis, True)) + jnp.pad(coupling, widths(axis, False))


def net_flow(flow, axis):
    return jnp.pad(flow, widths(axis, False)) - jnp.pad(flow, widths(axis, True))


def coefficients(perm, scale):
    couple_x = scale * harmonic(perm[1:], perm[:-1])
    couple_y = scale * harmonic(perm[:, 1:], perm[:, :-1])
    couple_z = harmonic(perm[:, :, 1:], perm[:, :, :-1])
    diagonal = STORE + face_sum(couple_x, 0) + face_sum(couple_y, 1) + face_sum(couple_z, 2)
    return (couple_x, couple_y, couple_z, diagonal)


def apply_operator(value, parts):
    couple_x, couple_y, couple_z, diagonal = parts
    flow_x = couple_x * (value[:-1] - value[1:])
    flow_y = couple_y * (value[:, :-1] - value[:, 1:])
    flow_z = couple_z * (value[:, :, :-1] - value[:, :, 1:])
    return STORE * value + net_flow(flow_x, 0) + net_flow(flow_y, 1) + net_flow(flow_z, 2)


def restrict(field):
    sx, sy, sz = field.shape
    return 0.25 * jnp.sum(field.reshape(sx // 2, 2, sy // 2, 2, sz), axis=(1, 3))


def trim(field):
    return field[1:-1, 1:-1]


def grid_pad(stacked):
    return with_halo(stacked, (("gx", 1), ("gy", 2)), 1)


def pad_single(field, pad_fn):
    return pad_fn(field[None])[0]


def smooth_zero(rhs, perm_padded, scale, sweeps, pad_fn):
    parts = coefficients(perm_padded, scale)
    diagonal = trim(parts[3])
    value = OMEGA * rhs / diagonal
    for step in range(sweeps - 1):
        padded = pad_single(value, pad_fn)
        value = value + OMEGA * (rhs - trim(apply_operator(padded, parts))) / diagonal
    return (value, parts)


def body(pressure_init, source, permeability):
    region = grid_pad(jnp.stack([permeability, pressure_init]))
    parts0 = coefficients(region[0], 1.0)
    diagonal0 = trim(parts0[3])
    padded = region[1]
    pressure = pressure_init
    for step in range(SWEEPS):
        if step > 0:
            padded = pad_single(pressure, grid_pad)
        pressure = pressure + OMEGA * (source - trim(apply_operator(padded, parts0))) / diagonal0
    resid0 = source - trim(apply_operator(pad_single(pressure, grid_pad), parts0))
    rhs_mid = restrict(resid0)
    perm_mid = restrict(permeability)
    correction_mid, parts1 = smooth_zero(
        rhs_mid, pad_single(perm_mid, grid_pad), 0.25, SWEEPS, grid_pad
    )
    resid1 = rhs_mid - trim(apply_operator(pad_single(correction_mid, grid_pad), parts1))
    rhs_coarse = restrict(resid1)
    perm_coarse = restrict(perm_mid)
    correction_coarse, unused = smooth_zero(
        rhs_coarse, pad_single(perm_coarse, grid_pad), 0.0625, COARSE, grid_pad
    )
    return (pressure, correction_mid, correction_coarse)


def solution(mesh):
    placed = (P("gx", "gy", None), P("gx", "gy", None), P("gx", "gy", None))
    return jax.shard_map(
        body,
        mesh=mesh,
        in_specs=placed,
        out_specs=(P("gx", "gy", None), P("gx", "gy", None), P("gx", "gy", None)),
        check_vma=False,
    )
```

profile of v0, /device:TPU:1, one launch (start us, length us, event | category | flops | bytes accessed | tf_op | source)
XLA Modules:
  0.0 159.4 jit_solution(12449114617759541596)
XLA Ops:
  1.5 4.5 %collective-permute-start = (f32[2,1,32,128]{3,2,1,0:T(8,128)S(1)}, f32[2,1,32,128]{3,2,1,0:T(8,128)S(1)}, u32[]{:S(2)}, u32[]{:S(2)}) collective-permute-start(f32[2,1,32,128]{3,2,1,0:T(8,128)S(1)} %get-tuple-element.19), channel_id=1, source_target_pairs={{0,8},{8,16},{16,24},{1,9},{9,17},{17,25},{2,10},{10,18},{18,26},{... | collective-permute-start | bytes 98312 | tf_op jit(solution)/shard_map/ppermute | solution.py:21
  8.2 3.6 %collective-permute-start.24 = (f32[1,1,8,128]{3,2,1,0:T(8,128)S(1)}, f32[1,1,8,128]{3,2,1,0:T(8,128)S(1)}, u32[]{:S(2)}, u32[]{:S(2)}) collective-permute-start(f32[1,1,8,128]{3,2,1,0:T(8,128)S(1)} %get-tuple-element.75), channel_id=1, source_target_pairs={{0,8},{8,16},{16,24},{1,9},{9,17},{17,25},{2,10},{10,18},{18,26},{... | collective-permute-start | bytes 12296 | tf_op jit(solution)/shard_map/ppermute | solution.py:21
  13.8 3.6 %collective-permute-start.12 = (f32[1,1,16,128]{3,2,1,0:T(8,128)S(1)}, f32[1,1,16,128]{3,2,1,0:T(8,128)S(1)}, u32[]{:S(2)}, u32[]{:S(2)}) collective-permute-start(f32[1,1,16,128]{3,2,1,0:T(8,128)S(1)} %get-tuple-element.51), channel_id=1, source_target_pairs={{0,8},{8,16},{16,24},{1,9},{9,17},{17,25},{2,10},{10,18},{18,26},{... | collective-permute-start | bytes 24584 | tf_op jit(solution)/shard_map/ppermute | solution.py:21
  19.4 3.1 %collective-permute-start.26 = (f32[1,6,1,128]{3,2,1,0:T(1,128)S(1)}, f32[1,6,1,128]{3,2,1,0:T(1,128)S(1)}, u32[]{:S(2)}, u32[]{:S(2)}) collective-permute-start(f32[1,6,1,128]{3,2,1,0:T(1,128)S(1)} %get-tuple-element.67), channel_id=1, source_target_pairs={{0,1},{1,2},{2,3},{3,4},{4,5},{5,6},{6,7},{8,9},{9,10},{10,11},{11... | collective-permute-start | bytes 9224 | tf_op jit(solution)/shard_map/ppermute | solution.py:21
  23.9 4.0 %collective-permute-start.2 = (f32[2,18,1,128]{3,2,1,0:T(1,128)S(1)}, f32[2,18,1,128]{3,2,1,0:T(1,128)S(1)}, u32[]{:S(2)}, u32[]{:S(2)}) collective-permute-start(f32[2,18,1,128]{3,2,1,0:T(1,128)S(1)} %get-tuple-element.17), channel_id=1, source_target_pairs={{0,1},{1,2},{2,3},{3,4},{4,5},{5,6},{6,7},{8,9},{9,10},{10,11},{11... | collective-permute-start | bytes 55304 | tf_op jit(solution)/shard_map/ppermute | solution.py:21
  29.3 4.7 %collective-permute-start.14 = (f32[1,10,1,128]{3,2,1,0:T(1,128)S(1)}, f32[1,10,1,128]{3,2,1,0:T(1,128)S(1)}, u32[]{:S(2)}, u32[]{:S(2)}) collective-permute-start(f32[1,10,1,128]{3,2,1,0:T(1,128)S(1)} %get-tuple-element.43), channel_id=1, source_target_pairs={{0,1},{1,2},{2,3},{3,4},{4,5},{5,6},{6,7},{8,9},{9,10},{10,11},{11... | collective-permute-start | bytes 15368 | tf_op jit(solution)/shard_map/ppermute | solution.py:21
  37.4 4.8 %collective-permute-start.4 = (f32[1,1,32,128]{3,2,1,0:T(8,128)S(1)}, f32[1,1,32,128]{3,2,1,0:T(8,128)S(1)}, u32[]{:S(2)}, u32[]{:S(2)}) collective-permute-start(f32[1,1,32,128]{3,2,1,0:T(8,128)S(1)} %get-tuple-element.31), channel_id=1, source_target_pairs={{0,8},{8,16},{16,24},{1,9},{9,17},{17,25},{2,10},{10,18},{18,26},{... | collective-permute-start | bytes 49160 | tf_op jit(solution)/shard_map/ppermute | solution.py:21
  44.1 3.1 %collective-permute-done.5 = f32[1,1,32,128]{3,2,1,0:T(8,128)S(1)} collective-permute-done((f32[1,1,32,128]{3,2,1,0:T(8,128)S(1)}, f32[1,1,32,128]{3,2,1,0:T(8,128)S(1)}, u32[]{:S(2)}, u32[]{:S(2)}) %collective-permute-start.5) | collective-permute-done | bytes 16416 | tf_op jit(solution)/shard_map/ppermute | solution.py:22
  47.2 5.2 %collective-permute-start.6 = (f32[1,18,1,128]{3,2,1,0:T(1,128)S(1)}, f32[1,18,1,128]{3,2,1,0:T(1,128)S(1)}, u32[]{:S(2)}, u32[]{:S(2)}) collective-permute-start(f32[1,18,1,128]{3,2,1,0:T(1,128)S(1)} %get-tuple-element.27), channel_id=1, source_target_pairs={{0,1},{1,2},{2,3},{3,4},{4,5},{5,6},{6,7},{8,9},{9,10},{10,11},{11... | collective-permute-start | bytes 27656 | tf_op jit(solution)/shard_map/ppermute | solution.py:21
  53.8 4.2 %collective-permute-done.7 = f32[1,18,1,128]{3,2,1,0:T(1,128)S(1)} collective-permute-done((f32[1,18,1,128]{3,2,1,0:T(1,128)S(1)}, f32[1,18,1,128]{3,2,1,0:T(1,128)S(1)}, u32[]{:S(2)}, u32[]{:S(2)}) %collective-permute-start.7) | collective-permute-done | bytes 9248 | tf_op jit(solution)/shard_map/ppermute | solution.py:22
  58.6 3.1 %collective-permute-start.8 = (f32[1,1,32,128]{3,2,1,0:T(8,128)S(1)}, f32[1,1,32,128]{3,2,1,0:T(8,128)S(1)}, u32[]{:S(2)}, u32[]{:S(2)}) collective-permute-start(f32[1,1,32,128]{3,2,1,0:T(8,128)S(1)} %get-tuple-element.29), channel_id=1, source_target_pairs={{0,8},{8,16},{16,24},{1,9},{9,17},{17,25},{2,10},{10,18},{18,26},{... | collective-permute-start | bytes 49160 | tf_op jit(solution)/shard_map/ppermute | solution.py:21
  63.8 3.0 %collective-permute-done.9 = f32[1,1,32,128]{3,2,1,0:T(8,128)S(1)} collective-permute-done((f32[1,1,32,128]{3,2,1,0:T(8,128)S(1)}, f32[1,1,32,128]{3,2,1,0:T(8,128)S(1)}, u32[]{:S(2)}, u32[]{:S(2)}) %collective-permute-start.9) | collective-permute-done | bytes 16416 | tf_op jit(solution)/shard_map/ppermute | solution.py:22
  66.8 4.5 %collective-permute-start.10 = (f32[1,18,1,128]{3,2,1,0:T(1,128)S(1)}, f32[1,18,1,128]{3,2,1,0:T(1,128)S(1)}, u32[]{:S(2)}, u32[]{:S(2)}) collective-permute-start(f32[1,18,1,128]{3,2,1,0:T(1,128)S(1)} %get-tuple-element.25), channel_id=1, source_target_pairs={{0,1},{1,2},{2,3},{3,4},{4,5},{5,6},{6,7},{8,9},{9,10},{10,11},{11... | collective-permute-start | bytes 27656 | tf_op jit(solution)/shard_map/ppermute | solution.py:21
  72.7 3.1 %collective-permute-done.11 = f32[1,18,1,128]{3,2,1,0:T(1,128)S(1)} collective-permute-done((f32[1,18,1,128]{3,2,1,0:T(1,128)S(1)}, f32[1,18,1,128]{3,2,1,0:T(1,128)S(1)}, u32[]{:S(2)}, u32[]{:S(2)}) %collective-permute-start.11) | collective-permute-done | bytes 9248 | tf_op jit(solution)/shard_map/ppermute | solution.py:22
  76.7 3.4 %collective-permute-start.16 = (f32[1,1,16,128]{3,2,1,0:T(8,128)S(1)}, f32[1,1,16,128]{3,2,1,0:T(8,128)S(1)}, u32[]{:S(2)}, u32[]{:S(2)}) collective-permute-start(f32[1,1,16,128]{3,2,1,0:T(8,128)S(1)} %get-tuple-element.49), channel_id=1, source_target_pairs={{0,8},{8,16},{16,24},{1,9},{9,17},{17,25},{2,10},{10,18},{18,26},{... | collective-permute-start | bytes 24584 | tf_op jit(solution)/shard_map/ppermute | solution.py:21
  82.0 3.0 %collective-permute-done.17 = f32[1,1,16,128]{3,2,1,0:T(8,128)S(1)} collective-permute-done((f32[1,1,16,128]{3,2,1,0:T(8,128)S(1)}, f32[1,1,16,128]{3,2,1,0:T(8,128)S(1)}, u32[]{:S(2)}, u32[]{:S(2)}) %collective-permute-start.17) | collective-permute-done | bytes 8224 | tf_op jit(solution)/shard_map/ppermute | solution.py:22
  85.0 2.7 %collective-permute-start.18 = (f32[1,10,1,128]{3,2,1,0:T(1,128)S(1)}, f32[1,10,1,128]{3,2,1,0:T(1,128)S(1)}, u32[]{:S(2)}, u32[]{:S(2)}) collective-permute-start(f32[1,10,1,128]{3,2,1,0:T(1,128)S(1)} %get-tuple-element.41), channel_id=1, source_target_pairs={{0,1},{1,2},{2,3},{3,4},{4,5},{5,6},{6,7},{8,9},{9,10},{10,11},{11... | collective-permute-start | bytes 15368 | tf_op jit(solution)/shard_map/ppermute | solution.py:21
  89.0 3.3 %collective-permute-done.19 = f32[1,10,1,128]{3,2,1,0:T(1,128)S(1)} collective-permute-done((f32[1,10,1,128]{3,2,1,0:T(1,128)S(1)}, f32[1,10,1,128]{3,2,1,0:T(1,128)S(1)}, u32[]{:S(2)}, u32[]{:S(2)}) %collective-permute-start.19) | collective-permute-done | bytes 5152 | tf_op jit(solution)/shard_map/ppermute | solution.py:22
  92.7 3.1 %collective-permute-start.20 = (f32[1,1,16,128]{3,2,1,0:T(8,128)S(1)}, f32[1,1,16,128]{3,2,1,0:T(8,128)S(1)}, u32[]{:S(2)}, u32[]{:S(2)}) collective-permute-start(f32[1,1,16,128]{3,2,1,0:T(8,128)S(1)} %get-tuple-element.47), channel_id=1, source_target_pairs={{0,8},{8,16},{16,24},{1,9},{9,17},{17,25},{2,10},{10,18},{18,26},{... | collective-permute-start | bytes 24584 | tf_op jit(solution)/shard_map/ppermute | solution.py:21
  97.9 2.9 %collective-permute-done.21 = f32[1,1,16,128]{3,2,1,0:T(8,128)S(1)} collective-permute-done((f32[1,1,16,128]{3,2,1,0:T(8,128)S(1)}, f32[1,1,16,128]{3,2,1,0:T(8,128)S(1)}, u32[]{:S(2)}, u32[]{:S(2)}) %collective-permute-start.21) | collective-permute-done | bytes 8224 | tf_op jit(solution)/shard_map/ppermute | solution.py:22
  100.8 4.5 %collective-permute-start.22 = (f32[1,10,1,128]{3,2,1,0:T(1,128)S(1)}, f32[1,10,1,128]{3,2,1,0:T(1,128)S(1)}, u32[]{:S(2)}, u32[]{:S(2)}) collective-permute-start(f32[1,10,1,128]{3,2,1,0:T(1,128)S(1)} %get-tuple-element.39), channel_id=1, source_target_pairs={{0,1},{1,2},{2,3},{3,4},{4,5},{5,6},{6,7},{8,9},{9,10},{10,11},{11... | collective-permute-start | bytes 15368 | tf_op jit(solution)/shard_map/ppermute | solution.py:21
  106.7 3.0 %collective-permute-done.23 = f32[1,10,1,128]{3,2,1,0:T(1,128)S(1)} collective-permute-done((f32[1,10,1,128]{3,2,1,0:T(1,128)S(1)}, f32[1,10,1,128]{3,2,1,0:T(1,128)S(1)}, u32[]{:S(2)}, u32[]{:S(2)}) %collective-permute-start.23) | collective-permute-done | bytes 5152 | tf_op jit(solution)/shard_map/ppermute | solution.py:22
  110.3 3.4 %collective-permute-start.28 = (f32[1,1,8,128]{3,2,1,0:T(8,128)S(1)}, f32[1,1,8,128]{3,2,1,0:T(8,128)S(1)}, u32[]{:S(2)}, u32[]{:S(2)}) collective-permute-start(f32[1,1,8,128]{3,2,1,0:T(8,128)S(1)} %get-tuple-element.73), channel_id=1, source_target_pairs={{0,8},{8,16},{16,24},{1,9},{9,17},{17,25},{2,10},{10,18},{18,26},{... | collective-permute-start | bytes 12296 | tf_op jit(solution)/shard_map/ppermute | solution.py:21
  115.6 3.0 %collective-permute-done.29 = f32[1,1,8,128]{3,2,1,0:T(8,128)S(1)} collective-permute-done((f32[1,1,8,128]{3,2,1,0:T(8,128)S(1)}, f32[1,1,8,128]{3,2,1,0:T(8,128)S(1)}, u32[]{:S(2)}, u32[]{:S(2)}) %collective-permute-start.29) | collective-permute-done | bytes 4128 | tf_op jit(solution)/shard_map/ppermute | solution.py:22
  122.5 3.3 %collective-permute-done.31 = f32[1,6,1,128]{3,2,1,0:T(1,128)S(1)} collective-permute-done((f32[1,6,1,128]{3,2,1,0:T(1,128)S(1)}, f32[1,6,1,128]{3,2,1,0:T(1,128)S(1)}, u32[]{:S(2)}, u32[]{:S(2)}) %collective-permute-start.31) | collective-permute-done | bytes 3104 | tf_op jit(solution)/shard_map/ppermute | solution.py:22
  126.1 3.1 %collective-permute-start.32 = (f32[1,1,8,128]{3,2,1,0:T(8,128)S(1)}, f32[1,1,8,128]{3,2,1,0:T(8,128)S(1)}, u32[]{:S(2)}, u32[]{:S(2)}) collective-permute-start(f32[1,1,8,128]{3,2,1,0:T(8,128)S(1)} %get-tuple-element.71), channel_id=1, source_target_pairs={{0,8},{8,16},{16,24},{1,9},{9,17},{17,25},{2,10},{10,18},{18,26},{... | collective-permute-start | bytes 12296 | tf_op jit(solution)/shard_map/ppermute | solution.py:21
  131.2 3.0 %collective-permute-done.33 = f32[1,1,8,128]{3,2,1,0:T(8,128)S(1)} collective-permute-done((f32[1,1,8,128]{3,2,1,0:T(8,128)S(1)}, f32[1,1,8,128]{3,2,1,0:T(8,128)S(1)}, u32[]{:S(2)}, u32[]{:S(2)}) %collective-permute-start.33) | collective-permute-done | bytes 4128 | tf_op jit(solution)/shard_map/ppermute | solution.py:22
  134.2 4.5 %collective-permute-start.34 = (f32[1,6,1,128]{3,2,1,0:T(1,128)S(1)}, f32[1,6,1,128]{3,2,1,0:T(1,128)S(1)}, u32[]{:S(2)}, u32[]{:S(2)}) collective-permute-start(f32[1,6,1,128]{3,2,1,0:T(1,128)S(1)} %get-tuple-element.63), channel_id=1, source_target_pairs={{0,1},{1,2},{2,3},{3,4},{4,5},{5,6},{6,7},{8,9},{9,10},{10,11},{11... | collective-permute-start | bytes 9224 | tf_op jit(solution)/shard_map/ppermute | solution.py:21
  140.0 3.0 %collective-permute-done.35 = f32[1,6,1,128]{3,2,1,0:T(1,128)S(1)} collective-permute-done((f32[1,6,1,128]{3,2,1,0:T(1,128)S(1)}, f32[1,6,1,128]{3,2,1,0:T(1,128)S(1)}, u32[]{:S(2)}, u32[]{:S(2)}) %collective-permute-start.35) | collective-permute-done | bytes 3104 | tf_op jit(solution)/shard_map/ppermute | solution.py:22
  143.3 3.4 %collective-permute-start.36 = (f32[1,1,8,128]{3,2,1,0:T(8,128)S(1)}, f32[1,1,8,128]{3,2,1,0:T(8,128)S(1)}, u32[]{:S(2)}, u32[]{:S(2)}) collective-permute-start(f32[1,1,8,128]{3,2,1,0:T(8,128)S(1)} %get-tuple-element.69), channel_id=1, source_target_pairs={{0,8},{8,16},{16,24},{1,9},{9,17},{17,25},{2,10},{10,18},{18,26},{... | collective-permute-start | bytes 12296 | tf_op jit(solution)/shard_map/ppermute | solution.py:21
  148.6 3.0 %collective-permute-done.37 = f32[1,1,8,128]{3,2,1,0:T(8,128)S(1)} collective-permute-done((f32[1,1,8,128]{3,2,1,0:T(8,128)S(1)}, f32[1,1,8,128]{3,2,1,0:T(8,128)S(1)}, u32[]{:S(2)}, u32[]{:S(2)}) %collective-permute-start.37) | collective-permute-done | bytes 4128 | tf_op jit(solution)/shard_map/ppermute | solution.py:22
  155.5 3.0 %collective-permute-done.39 = f32[1,6,1,128]{3,2,1,0:T(1,128)S(1)} collective-permute-done((f32[1,6,1,128]{3,2,1,0:T(1,128)S(1)}, f32[1,6,1,128]{3,2,1,0:T(1,128)S(1)}, u32[]{:S(2)}, u32[]{:S(2)}) %collective-permute-start.39) | collective-permute-done | bytes 3104 | tf_op jit(solution)/shard_map/ppermute | solution.py:22
  (135 shorter events, 44.7 us)
Async XLA Ops:
  1.5 21.1 %collective-permute-start = (f32[2,1,32,128]{3,2,1,0:T(8,128)S(1)}, f32[2,1,32,128]{3,2,1,0:T(8,128)S(1)}, u32[]{:S(2)}, u32[]{:S(2)}) collective-permute-start(f32[2,1,32,128]{3,2,1,0:T(8,128)S(1)} %get-tuple-element.19), channel_id=1, source_target_pairs={{0,8},{8,16},{16,24},{1,9},{9,17},{17,25},{2,10},{10,18},{18,26},{... | collective-permute-start | bytes 98312 | tf_op jit(solution)/shard_map/ppermute | solution.py:21
  6.0 17.9 %collective-permute-start.1 = (f32[2,1,32,128]{3,2,1,0:T(8,128)S(1)}, f32[2,1,32,128]{3,2,1,0:T(8,128)S(1)}, u32[]{:S(2)}, u32[]{:S(2)}) collective-permute-start(f32[2,1,32,128]{3,2,1,0:T(8,128)S(1)} %get-tuple-element.20), channel_id=1, source_target_pairs={{8,0},{16,8},{24,16},{9,1},{17,9},{25,17},{10,2},{18,10},{26,18},{... | collective-permute-start | bytes 98312 | tf_op jit(solution)/shard_map/ppermute | solution.py:22
  8.2 9.2 %collective-permute-start.24 = (f32[1,1,8,128]{3,2,1,0:T(8,128)S(1)}, f32[1,1,8,128]{3,2,1,0:T(8,128)S(1)}, u32[]{:S(2)}, u32[]{:S(2)}) collective-permute-start(f32[1,1,8,128]{3,2,1,0:T(8,128)S(1)} %get-tuple-element.75), channel_id=1, source_target_pairs={{0,8},{8,16},{16,24},{1,9},{9,17},{17,25},{2,10},{10,18},{18,26},{... | collective-permute-start | bytes 12296 | tf_op jit(solution)/shard_map/ppermute | solution.py:21
  11.9 7.5 %collective-permute-start.25 = (f32[1,1,8,128]{3,2,1,0:T(8,128)S(1)}, f32[1,1,8,128]{3,2,1,0:T(8,128)S(1)}, u32[]{:S(2)}, u32[]{:S(2)}) collective-permute-start(f32[1,1,8,128]{3,2,1,0:T(8,128)S(1)} %get-tuple-element.76), channel_id=1, source_target_pairs={{8,0},{16,8},{24,16},{9,1},{17,9},{25,17},{10,2},{18,10},{26,18},{... | collective-permute-start | bytes 12296 | tf_op jit(solution)/shard_map/ppermute | solution.py:22
  13.8 14.1 %collective-permute-start.12 = (f32[1,1,16,128]{3,2,1,0:T(8,128)S(1)}, f32[1,1,16,128]{3,2,1,0:T(8,128)S(1)}, u32[]{:S(2)}, u32[]{:S(2)}) collective-permute-start(f32[1,1,16,128]{3,2,1,0:T(8,128)S(1)} %get-tuple-element.51), channel_id=1, source_target_pairs={{0,8},{8,16},{16,24},{1,9},{9,17},{17,25},{2,10},{10,18},{18,26},{... | collective-permute-start | bytes 24584 | tf_op jit(solution)/shard_map/ppermute | solution.py:21
  17.5 11.8 %collective-permute-start.13 = (f32[1,1,16,128]{3,2,1,0:T(8,128)S(1)}, f32[1,1,16,128]{3,2,1,0:T(8,128)S(1)}, u32[]{:S(2)}, u32[]{:S(2)}) collective-permute-start(f32[1,1,16,128]{3,2,1,0:T(8,128)S(1)} %get-tuple-element.52), channel_id=1, source_target_pairs={{8,0},{16,8},{24,16},{9,1},{17,9},{25,17},{10,2},{18,10},{26,18},{... | collective-permute-start | bytes 24584 | tf_op jit(solution)/shard_map/ppermute | solution.py:22
  19.4 62.5 %collective-permute-start.26 = (f32[1,6,1,128]{3,2,1,0:T(1,128)S(1)}, f32[1,6,1,128]{3,2,1,0:T(1,128)S(1)}, u32[]{:S(2)}, u32[]{:S(2)}) collective-permute-start(f32[1,6,1,128]{3,2,1,0:T(1,128)S(1)} %get-tuple-element.67), channel_id=1, source_target_pairs={{0,1},{1,2},{2,3},{3,4},{4,5},{5,6},{6,7},{8,9},{9,10},{10,11},{11... | collective-permute-start | bytes 9224 | tf_op jit(solution)/shard_map/ppermute | solution.py:21
  22.6 59.4 %collective-permute-start.27 = (f32[1,6,1,128]{3,2,1,0:T(1,128)S(1)}, f32[1,6,1,128]{3,2,1,0:T(1,128)S(1)}, u32[]{:S(2)}, u32[]{:S(2)}) collective-permute-start(f32[1,6,1,128]{3,2,1,0:T(1,128)S(1)} %get-tuple-element.68), channel_id=1, source_target_pairs={{1,0},{2,1},{3,2},{4,3},{5,4},{6,5},{7,6},{9,8},{10,9},{11,10},{12... | collective-permute-start | bytes 9224 | tf_op jit(solution)/shard_map/ppermute | solution.py:22
  23.9 10.1 %collective-permute-start.2 = (f32[2,18,1,128]{3,2,1,0:T(1,128)S(1)}, f32[2,18,1,128]{3,2,1,0:T(1,128)S(1)}, u32[]{:S(2)}, u32[]{:S(2)}) collective-permute-start(f32[2,18,1,128]{3,2,1,0:T(1,128)S(1)} %get-tuple-element.17), channel_id=1, source_target_pairs={{0,1},{1,2},{2,3},{3,4},{4,5},{5,6},{6,7},{8,9},{9,10},{10,11},{11... | collective-permute-start | bytes 55304 | tf_op jit(solution)/shard_map/ppermute | solution.py:21
  27.9 7.4 %collective-permute-start.3 = (f32[2,18,1,128]{3,2,1,0:T(1,128)S(1)}, f32[2,18,1,128]{3,2,1,0:T(1,128)S(1)}, u32[]{:S(2)}, u32[]{:S(2)}) collective-permute-start(f32[2,18,1,128]{3,2,1,0:T(1,128)S(1)} %get-tuple-element.18), channel_id=1, source_target_pairs={{1,0},{2,1},{3,2},{4,3},{5,4},{6,5},{7,6},{9,8},{10,9},{11,10},{12... | collective-permute-start | bytes 55304 | tf_op jit(solution)/shard_map/ppermute | solution.py:22
  29.3 12.9 %collective-permute-start.14 = (f32[1,10,1,128]{3,2,1,0:T(1,128)S(1)}, f32[1,10,1,128]{3,2,1,0:T(1,128)S(1)}, u32[]{:S(2)}, u32[]{:S(2)}) collective-permute-start(f32[1,10,1,128]{3,2,1,0:T(1,128)S(1)} %get-tuple-element.43), channel_id=1, source_target_pairs={{0,1},{1,2},{2,3},{3,4},{4,5},{5,6},{6,7},{8,9},{9,10},{10,11},{11... | collective-permute-start | bytes 15368 | tf_op jit(solution)/shard_map/ppermute | solution.py:21
  34.0 10.1 %collective-permute-start.15 = (f32[1,10,1,128]{3,2,1,0:T(1,128)S(1)}, f32[1,10,1,128]{3,2,1,0:T(1,128)S(1)}, u32[]{:S(2)}, u32[]{:S(2)}) collective-permute-start(f32[1,10,1,128]{3,2,1,0:T(1,128)S(1)} %get-tuple-element.44), channel_id=1, source_target_pairs={{1,0},{2,1},{3,2},{4,3},{5,4},{6,5},{7,6},{9,8},{10,9},{11,10},{12... | collective-permute-start | bytes 15368 | tf_op jit(solution)/shard_map/ppermute | solution.py:22
  37.4 6.8 %collective-permute-start.4 = (f32[1,1,32,128]{3,2,1,0:T(8,128)S(1)}, f32[1,1,32,128]{3,2,1,0:T(8,128)S(1)}, u32[]{:S(2)}, u32[]{:S(2)}) collective-permute-start(f32[1,1,32,128]{3,2,1,0:T(8,128)S(1)} %get-tuple-element.31), channel_id=1, source_target_pairs={{0,8},{8,16},{16,24},{1,9},{9,17},{17,25},{2,10},{10,18},{18,26},{... | collective-permute-start | bytes 49160 | tf_op jit(solution)/shard_map/ppermute | solution.py:21
  42.1 5.1 %collective-permute-start.5 = (f32[1,1,32,128]{3,2,1,0:T(8,128)S(1)}, f32[1,1,32,128]{3,2,1,0:T(8,128)S(1)}, u32[]{:S(2)}, u32[]{:S(2)}) collective-permute-start(f32[1,1,32,128]{3,2,1,0:T(8,128)S(1)} %get-tuple-element.32), channel_id=1, source_target_pairs={{8,0},{16,8},{24,16},{9,1},{17,9},{25,17},{10,2},{18,10},{26,18},{... | collective-permute-start | bytes 49160 | tf_op jit(solution)/shard_map/ppermute | solution.py:22
  47.2 6.5 %collective-permute-start.6 = (f32[1,18,1,128]{3,2,1,0:T(1,128)S(1)}, f32[1,18,1,128]{3,2,1,0:T(1,128)S(1)}, u32[]{:S(2)}, u32[]{:S(2)}) collective-permute-start(f32[1,18,1,128]{3,2,1,0:T(1,128)S(1)} %get-tuple-element.27), channel_id=1, source_target_pairs={{0,1},{1,2},{2,3},{3,4},{4,5},{5,6},{6,7},{8,9},{9,10},{10,11},{11... | collective-permute-start | bytes 27656 | tf_op jit(solution)/shard_map/ppermute | solution.py:21
  52.4 5.6 %collective-permute-start.7 = (f32[1,18,1,128]{3,2,1,0:T(1,128)S(1)}, f32[1,18,1,128]{3,2,1,0:T(1,128)S(1)}, u32[]{:S(2)}, u32[]{:S(2)}) collective-permute-start(f32[1,18,1,128]{3,2,1,0:T(1,128)S(1)} %get-tuple-element.28), channel_id=1, source_target_pairs={{1,0},{2,1},{3,2},{4,3},{5,4},{6,5},{7,6},{9,8},{10,9},{11,10},{12... | collective-permute-start | bytes 27656 | tf_op jit(solution)/shard_map/ppermute | solution.py:22
  58.6 5.1 %collective-permute-start.8 = (f32[1,1,32,128]{3,2,1,0:T(8,128)S(1)}, f32[1,1,32,128]{3,2,1,0:T(8,128)S(1)}, u32[]{:S(2)}, u32[]{:S(2)}) collective-permute-start(f32[1,1,32,128]{3,2,1,0:T(8,128)S(1)} %get-tuple-element.29), channel_id=1, source_target_pairs={{0,8},{8,16},{16,24},{1,9},{9,17},{17,25},{2,10},{10,18},{18,26},{... | collective-permute-start | bytes 49160 | tf_op jit(solution)/shard_map/ppermute | solution.py:21
  61.7 5.1 %collective-permute-start.9 = (f32[1,1,32,128]{3,2,1,0:T(8,128)S(1)}, f32[1,1,32,128]{3,2,1,0:T(8,128)S(1)}, u32[]{:S(2)}, u32[]{:S(2)}) collective-permute-start(f32[1,1,32,128]{3,2,1,0:T(8,128)S(1)} %get-tuple-element.30), channel_id=1, source_target_pairs={{8,0},{16,8},{24,16},{9,1},{17,9},{25,17},{10,2},{18,10},{26,18},{... | collective-permute-start | bytes 49160 | tf_op jit(solution)/shard_map/ppermute | solution.py:22
  66.8 5.9 %collective-permute-start.10 = (f32[1,18,1,128]{3,2,1,0:T(1,128)S(1)}, f32[1,18,1,128]{3,2,1,0:T(1,128)S(1)}, u32[]{:S(2)}, u32[]{:S(2)}) collective-permute-start(f32[1,18,1,128]{3,2,1,0:T(1,128)S(1)} %get-tuple-element.25), channel_id=1, source_target_pairs={{0,1},{1,2},{2,3},{3,4},{4,5},{5,6},{6,7},{8,9},{9,10},{10,11},{11... | collective-permute-start | bytes 27656 | tf_op jit(solution)/shard_map/ppermute | solution.py:21
  76.7 5.3 %collective-permute-start.16 = (f32[1,1,16,128]{3,2,1,0:T(8,128)S(1)}, f32[1,1,16,128]{3,2,1,0:T(8,128)S(1)}, u32[]{:S(2)}, u32[]{:S(2)}) collective-permute-start(f32[1,1,16,128]{3,2,1,0:T(8,128)S(1)} %get-tuple-element.49), channel_id=1, source_target_pairs={{0,8},{8,16},{16,24},{1,9},{9,17},{17,25},{2,10},{10,18},{18,26},{... | collective-permute-start | bytes 24584 | tf_op jit(solution)/shard_map/ppermute | solution.py:21
  80.0 5.0 %collective-permute-start.17 = (f32[1,1,16,128]{3,2,1,0:T(8,128)S(1)}, f32[1,1,16,128]{3,2,1,0:T(8,128)S(1)}, u32[]{:S(2)}, u32[]{:S(2)}) collective-permute-start(f32[1,1,16,128]{3,2,1,0:T(8,128)S(1)} %get-tuple-element.50), channel_id=1, source_target_pairs={{8,0},{16,8},{24,16},{9,1},{17,9},{25,17},{10,2},{18,10},{26,18},{... | collective-permute-start | bytes 24584 | tf_op jit(solution)/shard_map/ppermute | solution.py:22
  87.7 4.6 %collective-permute-start.19 = (f32[1,10,1,128]{3,2,1,0:T(1,128)S(1)}, f32[1,10,1,128]{3,2,1,0:T(1,128)S(1)}, u32[]{:S(2)}, u32[]{:S(2)}) collective-permute-start(f32[1,10,1,128]{3,2,1,0:T(1,128)S(1)} %get-tuple-element.42), channel_id=1, source_target_pairs={{1,0},{2,1},{3,2},{4,3},{5,4},{6,5},{7,6},{9,8},{10,9},{11,10},{12... | collective-permute-start | bytes 15368 | tf_op jit(solution)/shard_map/ppermute | solution.py:22
  92.7 5.1 %collective-permute-start.20 = (f32[1,1,16,128]{3,2,1,0:T(8,128)S(1)}, f32[1,1,16,128]{3,2,1,0:T(8,128)S(1)}, u32[]{:S(2)}, u32[]{:S(2)}) collective-permute-start(f32[1,1,16,128]{3,2,1,0:T(8,128)S(1)} %get-tuple-element.47), channel_id=1, source_target_pairs={{0,8},{8,16},{16,24},{1,9},{9,17},{17,25},{2,10},{10,18},{18,26},{... | collective-permute-start | bytes 24584 | tf_op jit(solution)/shard_map/ppermute | solution.py:21
  95.8 5.0 %collective-permute-start.21 = (f32[1,1,16,128]{3,2,1,0:T(8,128)S(1)}, f32[1,1,16,128]{3,2,1,0:T(8,128)S(1)}, u32[]{:S(2)}, u32[]{:S(2)}) collective-permute-start(f32[1,1,16,128]{3,2,1,0:T(8,128)S(1)} %get-tuple-element.48), channel_id=1, source_target_pairs={{8,0},{16,8},{24,16},{9,1},{17,9},{25,17},{10,2},{18,10},{26,18},{... | collective-permute-start | bytes 24584 | tf_op jit(solution)/shard_map/ppermute | solution.py:22
  100.8 5.9 %collective-permute-start.22 = (f32[1,10,1,128]{3,2,1,0:T(1,128)S(1)}, f32[1,10,1,128]{3,2,1,0:T(1,128)S(1)}, u32[]{:S(2)}, u32[]{:S(2)}) collective-permute-start(f32[1,10,1,128]{3,2,1,0:T(1,128)S(1)} %get-tuple-element.39), channel_id=1, source_target_pairs={{0,1},{1,2},{2,3},{3,4},{4,5},{5,6},{6,7},{8,9},{9,10},{10,11},{11... | collective-permute-start | bytes 15368 | tf_op jit(solution)/shard_map/ppermute | solution.py:21
  110.3 5.3 %collective-permute-start.28 = (f32[1,1,8,128]{3,2,1,0:T(8,128)S(1)}, f32[1,1,8,128]{3,2,1,0:T(8,128)S(1)}, u32[]{:S(2)}, u32[]{:S(2)}) collective-permute-start(f32[1,1,8,128]{3,2,1,0:T(8,128)S(1)} %get-tuple-element.73), channel_id=1, source_target_pairs={{0,8},{8,16},{16,24},{1,9},{9,17},{17,25},{2,10},{10,18},{18,26},{... | collective-permute-start | bytes 12296 | tf_op jit(solution)/shard_map/ppermute | solution.py:21
  113.7 4.9 %collective-permute-start.29 = (f32[1,1,8,128]{3,2,1,0:T(8,128)S(1)}, f32[1,1,8,128]{3,2,1,0:T(8,128)S(1)}, u32[]{:S(2)}, u32[]{:S(2)}) collective-permute-start(f32[1,1,8,128]{3,2,1,0:T(8,128)S(1)} %get-tuple-element.74), channel_id=1, source_target_pairs={{8,0},{16,8},{24,16},{9,1},{17,9},{25,17},{10,2},{18,10},{26,18},{... | collective-permute-start | bytes 12296 | tf_op jit(solution)/shard_map/ppermute | solution.py:22
  126.1 5.0 %collective-permute-start.32 = (f32[1,1,8,128]{3,2,1,0:T(8,128)S(1)}, f32[1,1,8,128]{3,2,1,0:T(8,128)S(1)}, u32[]{:S(2)}, u32[]{:S(2)}) collective-permute-start(f32[1,1,8,128]{3,2,1,0:T(8,128)S(1)} %get-tuple-element.71), channel_id=1, source_target_pairs={{0,8},{8,16},{16,24},{1,9},{9,17},{17,25},{2,10},{10,18},{18,26},{... | collective-permute-start | bytes 12296 | tf_op jit(solution)/shard_map/ppermute | solution.py:21
  129.2 4.9 %collective-permute-start.33 = (f32[1,1,8,128]{3,2,1,0:T(8,128)S(1)}, f32[1,1,8,128]{3,2,1,0:T(8,128)S(1)}, u32[]{:S(2)}, u32[]{:S(2)}) collective-permute-start(f32[1,1,8,128]{3,2,1,0:T(8,128)S(1)} %get-tuple-element.72), channel_id=1, source_target_pairs={{8,0},{16,8},{24,16},{9,1},{17,9},{25,17},{10,2},{18,10},{26,18},{... | collective-permute-start | bytes 12296 | tf_op jit(solution)/shard_map/ppermute | solution.py:22
  134.2 5.8 %collective-permute-start.34 = (f32[1,6,1,128]{3,2,1,0:T(1,128)S(1)}, f32[1,6,1,128]{3,2,1,0:T(1,128)S(1)}, u32[]{:S(2)}, u32[]{:S(2)}) collective-permute-start(f32[1,6,1,128]{3,2,1,0:T(1,128)S(1)} %get-tuple-element.63), channel_id=1, source_target_pairs={{0,1},{1,2},{2,3},{3,4},{4,5},{5,6},{6,7},{8,9},{9,10},{10,11},{11... | collective-permute-start | bytes 9224 | tf_op jit(solution)/shard_map/ppermute | solution.py:21
  143.3 5.3 %collective-permute-start.36 = (f32[1,1,8,128]{3,2,1,0:T(8,128)S(1)}, f32[1,1,8,128]{3,2,1,0:T(8,128)S(1)}, u32[]{:S(2)}, u32[]{:S(2)}) collective-permute-start(f32[1,1,8,128]{3,2,1,0:T(8,128)S(1)} %get-tuple-element.69), channel_id=1, source_target_pairs={{0,8},{8,16},{16,24},{1,9},{9,17},{17,25},{2,10},{10,18},{18,26},{... | collective-permute-start | bytes 12296 | tf_op jit(solution)/shard_map/ppermute | solution.py:21
  146.7 4.9 %collective-permute-start.37 = (f32[1,1,8,128]{3,2,1,0:T(8,128)S(1)}, f32[1,1,8,128]{3,2,1,0:T(8,128)S(1)}, u32[]{:S(2)}, u32[]{:S(2)}) collective-permute-start(f32[1,1,8,128]{3,2,1,0:T(8,128)S(1)} %get-tuple-element.70), channel_id=1, source_target_pairs={{8,0},{16,8},{24,16},{9,1},{17,9},{25,17},{10,2},{18,10},{26,18},{... | collective-permute-start | bytes 12296 | tf_op jit(solution)/shard_map/ppermute | solution.py:22
  (13 other events, 92.0 us)
where the time goes:
time: 161 us; the launch traced here: 159 us
  starting transfers between devices  106 us (66%)
  waiting for transfers between devices  44 us (27%)
  other arithmetic  6.34 us (4%)
    ppermute x20, starting transfers between devices, with_halo(): before = lax.ppermute(last, axis, up)  74.3 us
    ppermute x20, waiting for transfers between devices, with_halo(): after = lax.ppermute(leading, axis, down)  44 us
    ppermute x20, starting transfers between devices, with_halo(): after = lax.ppermute(leading, axis, down)  32.1 us
  transfers between devices with their start and end apart: 40, of which 14 were waited for; matrix products, arithmetic and copies ran while one was open for 2% of the time, Pallas kernels for 0%

commit v1 on v0

v1 whole, which is shorter than its diff:
```python
import functools

import jax
import jax.numpy as jnp
from jax import lax
from jax.experimental import pallas as pl
from jax.experimental.pallas import tpu as pltpu
from jax.sharding import PartitionSpec as P

STORE = 0.1
OMEGA = 0.8
MESH = pl.DeviceIdType.MESH
DIRS = ((-1, 0), (1, 0), (0, -1), (0, 1), (-1, -1), (-1, 1), (1, -1), (1, 1))
CHUNK = 2


def hm(a, b):
    return 2.0 * a * b / jnp.maximum(a + b, 1e-30)


def over_planes(lo, hi, fn, chunk=CHUNK):
    whole = (hi - lo) // chunk

    def step(t, carry):
        fn(lo + t * chunk, chunk)
        return carry

    if whole:
        lax.fori_loop(0, whole, step, 0)
    if (hi - lo) % chunk:
        fn(lo + whole * chunk, (hi - lo) % chunk)


def rolls(rows):
    def y_next(v):
        return pltpu.roll(v, rows - 1, 1)

    def y_prev(v):
        return pltpu.roll(v, 1, 1)

    def z_next(v):
        return pltpu.roll(v, 127, 2)

    def z_prev(v):
        return pltpu.roll(v, 1, 2)

    return y_next, y_prev, z_next, z_prev


def make_coefficients(k, cx, cy, cz, w, d, scale):
    planes, rows, _ = k.shape
    y_next, y_prev, z_next, z_prev = rolls(rows)
    cx[0] = scale * hm(k[0], k[1])

    def fn(i, n):
        here = k[pl.ds(i, n)]
        x = scale * hm(here, k[pl.ds(i + 1, n)])
        cx[pl.ds(i, n)] = x
        y = scale * hm(here, y_next(here))
        cy[pl.ds(i, n)] = y
        z = hm(here, z_next(here))
        lane = lax.broadcasted_iota(jnp.int32, z.shape, 2)
        z = jnp.where(lane < 127, z, 0.0)
        cz[pl.ds(i, n)] = z
        diag = STORE + x + cx[pl.ds(i - 1, n)] + y + y_prev(y) + z + z_prev(z)
        d[pl.ds(i, n)] = diag
        w[pl.ds(i, n)] = OMEGA / diag

    over_planes(1, planes - 1, fn)


def neighbour_sum(v, cx, cy, cz, i, n):
    y_next, y_prev, z_next, z_prev = rolls(v.shape[1])
    here = v[pl.ds(i, n)]
    y = cy[pl.ds(i, n)]
    z = cz[pl.ds(i, n)]
    total = cx[pl.ds(i, n)] * v[pl.ds(i + 1, n)] + cx[pl.ds(i - 1, n)] * v[pl.ds(i - 1, n)]
    total = total + (y * y_next(here) + y_prev(y * here))
    total = total + (z * z_next(here) + z_prev(z * here))
    return here, total


def sweep(src, dst, b, cx, cy, cz, w, lo, hi):
    def fn(i, n):
        here, total = neighbour_sum(src, cx, cy, cz, i, n)
        dst[pl.ds(i, n)] = (1.0 - OMEGA) * here + w[pl.ds(i, n)] * (b[pl.ds(i, n)] + total)

    over_planes(lo, hi, fn)


def restrict(src, off, tmp, dst, dst_off, cx_, cy_):
    for i in range(cx_):
        tmp[i] = 0.25 * (src[off + 2 * i, 0 : 2 * cy_] + src[off + 2 * i + 1, 0 : 2 * cy_])
        dst[dst_off + i, 0:cy_] = tmp[i, pl.ds(0, cy_, stride=2)] + tmp[i, pl.ds(1, cy_, stride=2)]


def edge_rows(extent, width, step):
    return range(extent - width, extent) if step > 0 else range(width)


def halo_rows(extent, rows, width, step):
    return range(rows - width, rows) if step > 0 else range(extent, extent + width)


def halo_planes(extent, off, width, step):
    return range(off - width, off) if step > 0 else range(off + extent, off + extent + width)


def flat(ref):
    planes, rows, lanes = ref.shape
    return ref.reshape(planes * rows, lanes)


def zero_halo(ref, extent_x, extent_y, off):
    planes, rows, lanes = ref.shape
    ref[0:off] = jnp.zeros((off, rows, lanes), jnp.float32)
    ref[off + extent_x : planes] = jnp.zeros((planes - off - extent_x, rows, lanes), jnp.float32)
    ref[off : off + extent_x, extent_y:rows] = jnp.zeros((extent_x, rows - extent_y, lanes), jnp.float32)


def kernel(
    p_in, s_in, k_in, p_out, c1_out, c2_out,
    k0, p0, s0, p1, p2, cx0, cy0, cz0, w0, d0,
    k1, b1, u1, v1, cx1, cy1, cz1, w1, d1,
    k2, b2, u2, v2, cx2, cy2, cz2, w2, d2,
    r0, r1, t0, t1,
    ya, yar, ca, car, yb, ybr, cb, cbr, yc, ycr, cc, ccr, yd, ydr, cd, cdr,
    lsem, ssem, rsem,
):
    X, Y = p_in.shape[0], p_in.shape[1]
    nx, ny = lax.axis_size("gx"), lax.axis_size("gy")
    gx, gy = lax.axis_index("gx"), lax.axis_index("gy")
    H0, H1, H2 = 3, 3, 4
    X1, Y1, X2, Y2 = X // 2, Y // 2, X // 4, Y // 4

    def exists(d):
        dx, dy = d
        ok = None
        for coord, step, size in ((gx, dx, nx), (gy, dy, ny)):
            if step:
                one = (coord + step >= 0) & (coord + step < size)
                ok = one if ok is None else ok & one
        return ok

    here = {d: exists(d) for d in DIRS}

    def opposite(d):
        return (-d[0], -d[1])

    local = [
        pltpu.make_async_copy(src, dst.at[H0 : H0 + X, 0:Y], lsem.at[i])
        for i, (src, dst) in enumerate(((k_in, k0), (p_in, p0), (s_in, s0)))
    ]
    for copy in local:
        copy.start()
    for ref in (k0, p0, s0):
        zero_halo(ref, X, Y, H0)
    for ref in (k1, b1):
        zero_halo(ref, X1, Y1, H1)
    for ref in (k2, b2):
        zero_halo(ref, X2, Y2, H2)

    barrier = pltpu.get_barrier_semaphore()
    for d in DIRS:

        @pl.when(here[d])
        def _():
            pl.semaphore_signal(
                barrier, inc=1, device_id={"gx": gx + d[0], "gy": gy + d[1]}, device_id_type=MESH
            )

    one = lambda d: here[d].astype(jnp.int32)
    count = one(DIRS[0])
    for d in DIRS[1:]:
        count = count + one(d)
    pl.semaphore_wait(barrier, count)

    counter = [0]
    every = []

    def message(d, src, dst):
        slot = counter[0]
        counter[0] += 1
        copy = pltpu.make_async_remote_copy(
            src_ref=src, dst_ref=dst, send_sem=ssem.at[slot], recv_sem=rsem.at[slot],
            device_id={"gx": gx + d[0], "gy": gy + d[1]}, device_id_type=MESH,
        )

        @pl.when(here[d])
        def _():
            copy.start()

        every.append((d, copy))
        return d, copy

    def receive(messages):
        for d, copy in messages:

            @pl.when(here[opposite(d)])
            def _():
                copy.wait_recv()

    def part(ref, planes, rows):
        return ref.at[planes.start : planes.stop, 0:rows]

    def tile_planes(extent, width, step):
        edge = edge_rows(extent, width, step)
        return edge

    sent_a = []
    for d in ((-1, 0), (1, 0)):
        for src, dst, width in ((k_in, k0, 3), (p_in, p0, 3), (s_in, s0, 2)):
            planes = edge_rows(X, width, d[0])
            sent_a.append(
                message(d, src.at[planes.start : planes.stop], part(dst, halo_planes(X, H0, width, d[0]), Y))
            )
    for copy in local:
        copy.wait()
    R0, R1, R2 = k0.shape[1], k1.shape[1], k2.shape[1]
    arrays_a = ((k0, 3), (p0, 3), (s0, 2))
    for j, dy in enumerate((-1, 1)):
        slot = 0
        for ref, width in arrays_a:
            for y in edge_rows(Y, width, dy):
                ya[j, slot] = flat(ref)[pl.ds(H0 * R0 + y, X, stride=R0), :]
                slot += 1
        sent_a.append(message((0, dy), ya.at[j], yar.at[j]))

    def pack_corner(stage, j, slot, ref, off, ex, ey, width, d):
        ys = edge_rows(ey, width, d[1])
        for x in edge_rows(ex, width, d[0]):
            stage[j, slot : slot + width] = ref[off + x, ys.start : ys.stop]
            slot += width
        return slot

    def unpack_corner(stage, j, slot, ref, off, ex, ey, width, d):
        ys = halo_rows(ey, ref.shape[1], width, d[1])
        for x in halo_planes(ex, off, width, d[0]):
            ref[x, ys.start : ys.stop] = stage[j, slot : slot + width]
            slot += width
        return slot

    corners_a = ((k0, 2), (p0, 2), (s0, 1))
    for j, d in enumerate(DIRS[4:]):
        slot = 0
        for ref, width in corners_a:
            slot = pack_corner(ca, j, slot, ref, H0, X, Y, width, d)
        sent_a.append(message(d, ca.at[j], car.at[j]))

    restrict(k0, H0, t0, k1, H1, X1, Y1)
    restrict(k1, H1, t1, k2, H2, X2, Y2)
    sent_b = []
    for d in ((-1, 0), (1, 0)):
        for ref, off, ex, ey, width in ((k1, H1, X1, Y1, 3), (k2, H2, X2, Y2, 4)):
            planes = edge_rows(ex, width, d[0])
            src = ref.at[off + planes.start : off + planes.stop, 0:ey]
            sent_b.append(message(d, src, part(ref, halo_planes(ex, off, width, d[0]), ey)))
    for j, dy in enumerate((-1, 1)):
        slot = 0
        for y in edge_rows(Y1, 3, dy):
            yb[j, slot : slot + X1] = flat(k1)[pl.ds(H1 * R1 + y, X1, stride=R1), :]
            slot += X1
        for y in edge_rows(Y2, 4, dy):
            yb[j, slot : slot + X2] = flat(k2)[pl.ds(H2 * R2 + y, X2, stride=R2), :]
            slot += X2
        sent_b.append(message((0, dy), yb.at[j], ybr.at[j]))
    for j, d in enumerate(DIRS[4:]):
        slot = pack_corner(cb, j, 0, k1, H1, X1, Y1, 2, d)
        pack_corner(cb, j, slot, k2, H2, X2, Y2, 3, d)
        sent_b.append(message(d, cb.at[j], cbr.at[j]))

    receive(sent_a)
    for j, dy in enumerate((-1, 1)):

        @pl.when(here[(0, -dy)])
        def _():
            slot = 0
            for ref, width in arrays_a:
                for y in halo_rows(Y, R0, width, dy):
                    flat(ref)[pl.ds(H0 * R0 + y, X, stride=R0), :] = yar[j, slot]
                    slot += 1

    for j, d in enumerate(DIRS[4:]):

        @pl.when(here[opposite(d)])
        def _():
            slot = 0
            for ref, width in corners_a:
                slot = unpack_corner(car, j, slot, ref, H0, X, Y, width, d)

    make_coefficients(k0, cx0, cy0, cz0, w0, d0, 1.0)
    sweep(p0, p1, s0, cx0, cy0, cz0, w0, 1, X + 5)
    sweep(p1, p2, s0, cx0, cy0, cz0, w0, 2, X + 4)

    def residual0(i, n):
        value, total = neighbour_sum(p2, cx0, cy0, cz0, i, n)
        p_out[pl.ds(i - H0, n)] = value[:, 0:Y]
        r = s0[pl.ds(i, n)] + total - d0[pl.ds(i, n)] * value
        r0[pl.ds(i - H0, n)] = r[:, 0:Y]

    over_planes(H0, H0 + X, residual0)
    restrict(r0, 0, t0, b1, H1, X1, Y1)

    sent_c = []
    for d in ((-1, 0), (1, 0)):
        planes = edge_rows(X1, 2, d[0])
        src = b1.at[H1 + planes.start : H1 + planes.stop, 0:Y1]
        sent_c.append(message(d, src, part(b1, halo_planes(X1, H1, 2, d[0]), Y1)))
    for j, dy in enumerate((-1, 1)):
        for slot, y in enumerate(edge_rows(Y1, 2, dy)):
            yc[j, slot] = flat(b1)[pl.ds(H1 * R1 + y, X1, stride=R1), :]
        sent_c.append(message((0, dy), yc.at[j], ycr.at[j]))
    for j, d in enumerate(DIRS[4:]):
        pack_corner(cc, j, 0, b1, H1, X1, Y1, 1, d)
        sent_c.append(message(d, cc.at[j], ccr.at[j]))

    receive(sent_b)
    for j, dy in enumerate((-1, 1)):

        @pl.when(here[(0, -dy)])
        def _():
            slot = 0
            for y in halo_rows(Y1, R1, 3, dy):
                flat(k1)[pl.ds(H1 * R1 + y, X1, stride=R1), :] = ybr[j, slot : slot + X1]
                slot += X1
            for y in halo_rows(Y2, R2, 4, dy):
                flat(k2)[pl.ds(H2 * R2 + y, X2, stride=R2), :] = ybr[j, slot : slot + X2]
                slot += X2

    for j, d in enumerate(DIRS[4:]):

        @pl.when(here[opposite(d)])
        def _():
            slot = unpack_corner(cbr, j, 0, k1, H1, X1, Y1, 2, d)
            unpack_corner(cbr, j, slot, k2, H2, X2, Y2, 3, d)

    make_coefficients(k1, cx1, cy1, cz1, w1, d1, 0.25)
    make_coefficients(k2, cx2, cy2, cz2, w2, d2, 0.0625)

    receive(sent_c)
    for j, dy in enumerate((-1, 1)):

        @pl.when(here[(0, -dy)])
        def _():
            for slot, y in enumerate(halo_rows(Y1, R1, 2, dy)):
                flat(b1)[pl.ds(H1 * R1 + y, X1, stride=R1), :] = ycr[j, slot]

    for j, d in enumerate(DIRS[4:]):

        @pl.when(here[opposite(d)])
        def _():
            unpack_corner(ccr, j, 0, b1, H1, X1, Y1, 1, d)

    u1[1 : X1 + 5] = w1[1 : X1 + 5] * b1[1 : X1 + 5]
    sweep(u1, v1, b1, cx1, cy1, cz1, w1, 2, X1 + 4)

    def residual1(i, n):
        value, total = neighbour_sum(v1, cx1, cy1, cz1, i, n)
        c1_out[pl.ds(i - H1, n)] = value[:, 0:Y1]
        r = b1[pl.ds(i, n)] + total - d1[pl.ds(i, n)] * value
        r1[pl.ds(i - H1, n)] = r[:, 0:Y1]

    over_planes(H1, H1 + X1, residual1)
    restrict(r1, 0, t1, b2, H2, X2, Y2)

    sent_d = []
    for d in ((-1, 0), (1, 0)):
        planes = edge_rows(X2, 3, d[0])
        src = b2.at[H2 + planes.start : H2 + planes.stop, 0:Y2]
        sent_d.append(message(d, src, part(b2, halo_planes(X2, H2, 3, d[0]), Y2)))
    for j, dy in enumerate((-1, 1)):
        for slot, y in enumerate(edge_rows(Y2, 3, dy)):
            yd[j, slot * X2 : slot * X2 + X2] = flat(b2)[pl.ds(H2 * R2 + y, X2, stride=R2), :]
        sent_d.append(message((0, dy), yd.at[j], ydr.at[j]))
    for j, d in enumerate(DIRS[4:]):
        pack_corner(cd, j, 0, b2, H2, X2, Y2, 2, d)
        sent_d.append(message(d, cd.at[j], cdr.at[j]))
    receive(sent_d)
    for j, dy in enumerate((-1, 1)):

        @pl.when(here[(0, -dy)])
        def _():
            for slot, y in enumerate(halo_rows(Y2, R2, 3, dy)):
                flat(b2)[pl.ds(H2 * R2 + y, X2, stride=R2), :] = ydr[j, slot * X2 : slot * X2 + X2]

    for j, d in enumerate(DIRS[4:]):

        @pl.when(here[opposite(d)])
        def _():
            unpack_corner(cdr, j, 0, b2, H2, X2, Y2, 2, d)

    u2[1 : X2 + 7] = w2[1 : X2 + 7] * b2[1 : X2 + 7]
    sweep(u2, v2, b2, cx2, cy2, cz2, w2, 2, X2 + 6)
    sweep(v2, u2, b2, cx2, cy2, cz2, w2, 3, X2 + 5)
    value, total = neighbour_sum(u2, cx2, cy2, cz2, H2, X2)
    value = (1.0 - OMEGA) * value + w2[H2 : H2 + X2] * (b2[H2 : H2 + X2] + total)
    c2_out[...] = value[:, 0:Y2]

    for d, copy in every:

        @pl.when(here[d])
        def _():
            copy.wait_send()


MESSAGES = 12 + 10 + 8 + 8


def body(pressure_init, source, permeability):
    X, Y, Z = permeability.shape
    f32 = jnp.float32

    def vmem(*shape):
        return pltpu.VMEM(shape, f32)

    def level(x, y, off):
        return (x + 2 * off, y + 8, Z)

    l0, l1, l2 = level(X, Y, 3), level(X // 2, Y // 2, 3), level(X // 4, Y // 4, 4)
    scratch = (
        [vmem(*l0)] * 10
        + [vmem(*l1)] * 9
        + [vmem(*l2)] * 9
        + [vmem(X, Y, Z), vmem(X // 2, Y // 2, Z), vmem(X // 2, Y, Z), vmem(X // 4, Y // 2, Z)]
        + [vmem(2, 8, X, Z)] * 2
        + [vmem(4, 16, Z)] * 2
        + [vmem(2, 3 * (X // 2) + 4 * (X // 4), Z)] * 2
        + [vmem(4, 16, Z)] * 2
        + [vmem(2, 2, X // 2, Z)] * 2
        + [vmem(4, 8, Z)] * 2
        + [vmem(2, 16, Z)] * 2
        + [vmem(4, 8, Z)] * 2
        + [
            pltpu.SemaphoreType.DMA((3,)),
            pltpu.SemaphoreType.DMA((MESSAGES,)),
            pltpu.SemaphoreType.DMA((MESSAGES,)),
        ]
    )
    return pl.pallas_call(
        kernel,
        out_shape=(
            jax.ShapeDtypeStruct((X, Y, Z), f32),
            jax.ShapeDtypeStruct((X // 2, Y // 2, Z), f32),
            jax.ShapeDtypeStruct((X // 4, Y // 4, Z), f32),
        ),
        in_specs=[pl.BlockSpec(memory_space=pl.ANY)] * 3,
        out_specs=[pl.BlockSpec(memory_space=pltpu.VMEM)] * 3,
        scratch_shapes=scratch,
        compiler_params=pltpu.CompilerParams(
            collective_id=0, has_side_effects=True, vmem_limit_bytes=32 * 1024 * 1024
        ),
    )(pressure_init, source, permeability)


def solution(mesh):
    spec = P("gx", "gy", None)
    return jax.shard_map(
        body, mesh=mesh, in_specs=(spec,) * 3, out_specs=(spec,) * 3, check_vma=False
    )
```

time: 161 us -> 29 us (0.18)
  starting transfers between devices: 106 us -> 0 us
  waiting for transfers between devices: 44 us -> 0 us
  Pallas kernels: 0 us -> 23.4 us
  other arithmetic: 6.34 us -> 0 us
  local copies, waits for them, and re-layouts: 0.94 us -> 4.78 us
    ppermute x40 -> x0, starting transfers between devices: 106 us -> none  [the longest x20 74.3 us: with_halo(): before = lax.ppermute(last, axis, up)]
    ppermute x40 -> x0, waiting for transfers between devices: 44 us -> none  [the longest x20 44 us: with_halo(): after = lax.ppermute(leading, axis, down)]
    pallas_call x0 -> x1, Pallas kernels: none -> 23.4 us  [body(): pl.pallas_call(kernel, out_shape=(jax.ShapeDtypeStruct((X, Y, Z), f32), j...]
    unnamed x10 -> x9, local copies, waits for them, and re-layouts: 0.85 us -> 4.78 us
    mul x30 -> x0, other arithmetic: 2.14 us -> none  [the longest x8 1.14 us: apply_operator(): flow_z = couple_z * (value[:, :, :-1] - value[:, :, 1:])]
    add x6 -> x0, other arithmetic: 1.75 us -> none  [the longest x4 0.96 us: smooth_zero(): value + OMEGA * (rhs - trim(apply_operator(padded, parts))) / diagonal]
  transfers between devices with their start and end apart: 40 -> 0, of which waited for: 14 -> 0; matrix products, arithmetic and copies ran while one was open for 2% -> 0% of each run, Pallas kernels for 0% -> 0%
where the time goes in v1:
time: 29 us; the launch traced here: 28.8 us
  Pallas kernels  23.4 us (81%)
  local copies, waits for them, and re-layouts  4.78 us (16%)
  between operations  0.65 us (2%)
    pallas_call x1, Pallas kernels, body(): pl.pallas_call(kernel, out_shape=(jax.ShapeDtypeStruct((X, Y, Z), f32), j...  23.4 us
    unnamed x9, local copies, waits for them, and re-layouts  4.78 us

profile of v1, /device:TPU:1, one launch (start us, length us, event | category | flops | bytes accessed | tf_op | source)
XLA Modules:
  0.0 28.8 jit_solution(18059247710934025249)
XLA Ops:
  0.6 0.0 copy-start
  0.6 0.9 %copy-done = f32[16,32,128]{2,1,0:T(8,128)S(1)} copy-done((f32[16,32,128]{2,1,0:T(8,128)S(1)}, f32[16,32,128]{2,1,0:T(8,128)}, u32[]{:S(2)}) %copy-start) | copy-done | bytes 262168
  1.6 0.0 copy-start.1
  1.6 0.9 %copy-done.1 = f32[16,32,128]{2,1,0:T(8,128)S(1)} copy-done((f32[16,32,128]{2,1,0:T(8,128)S(1)}, f32[16,32,128]{2,1,0:T(8,128)}, u32[]{:S(2)}) %copy-start.1) | copy-done | bytes 262168
  2.5 0.0 copy-start.2
  2.5 0.9 %copy-done.2 = f32[16,32,128]{2,1,0:T(8,128)S(1)} copy-done((f32[16,32,128]{2,1,0:T(8,128)S(1)}, f32[16,32,128]{2,1,0:T(8,128)}, u32[]{:S(2)}) %copy-start.2) | copy-done | bytes 262168
  3.5 23.4 %shard_map.58 = (f32[16,32,128]{2,1,0:T(8,128)S(1)}, f32[8,16,128]{2,1,0:T(8,128)S(1)}, f32[4,8,128]{2,1,0:T(8,128)S(1)}) custom-call(f32[16,32,128]{2,1,0:T(8,128)S(1)} %copy-done, f32[16,32,128]{2,1,0:T(8,128)S(1)} %copy-done.1, f32[16,32,128]{2,1,0:T(8,128)S(1)} %copy-done.2), custom_call_target="tpu_custom_call" | custom-call | tf_op jit(solution)/shard_map/pallas_call | solution.py:439
  26.9 0.7 %copy.9 = f32[16,32,128]{2,1,0:T(8,128)} copy(f32[16,32,128]{2,1,0:T(8,128)S(1)} %get-tuple-element.6) | data formatting | bytes 524288
  27.6 0.6 %copy.10 = f32[8,16,128]{2,1,0:T(8,128)} copy(f32[8,16,128]{2,1,0:T(8,128)S(1)} %get-tuple-element.7) | data formatting | bytes 131072
  28.2 0.6 %copy.11 = f32[4,8,128]{2,1,0:T(8,128)} copy(f32[4,8,128]{2,1,0:T(8,128)S(1)} %get-tuple-element.8) | data formatting | bytes 32768
Async XLA Ops:
  0.6 1.0 %copy-start = (f32[16,32,128]{2,1,0:T(8,128)S(1)}, f32[16,32,128]{2,1,0:T(8,128)}, u32[]{:S(2)}) copy-start(f32[16,32,128]{2,1,0:T(8,128)} %p_in.1) | copy-start | bytes 786436
  1.6 0.9 %copy-start.1 = (f32[16,32,128]{2,1,0:T(8,128)S(1)}, f32[16,32,128]{2,1,0:T(8,128)}, u32[]{:S(2)}) copy-start(f32[16,32,128]{2,1,0:T(8,128)} %s_in.1) | copy-start | bytes 786436
  2.5 0.9 %copy-start.2 = (f32[16,32,128]{2,1,0:T(8,128)S(1)}, f32[16,32,128]{2,1,0:T(8,128)}, u32[]{:S(2)}) copy-start(f32[16,32,128]{2,1,0:T(8,128)} %k_in.1) | copy-start | bytes 786436
